TPU v7x, 32 devices: a whole 2x2x4 slice. The times are simulated.
32 devices in a mesh: groups: 2 (over y), dev: 4 (over z), cuts: 4 (over x, core).
Axes of the slice: x: 2, y: 2, z: 4, core: 2. Of those that a mesh axis runs over, the one named last changes fastest.
Arguments:
- residual: bfloat16 [128, 3072], P(('groups', 'dev'), 'cuts'), parts along dimension 0, may hold values from -64 to 64
- queries: bfloat16 [128, 3072], P(('groups', 'dev'), 'cuts'), parts along dimension 0, may hold values from -30 to 30
- keys: bfloat16 [128, 32, 512], P(('groups', 'dev'), None, 'cuts'), parts along dimension 0, may hold values from -12 to 12
- values: bfloat16 [128, 32, 512], P(('groups', 'dev'), None, 'cuts'), parts along dimension 0, may hold values from -12 to 12
- lengths: int32 [128], P(('groups', 'dev')), parts along dimension 0, may hold values from 2 to 32, as said below
- norm_gain: float32 [3072], P('cuts'), may hold values from 0.1 to 1.9
- expert_ids: int32 [128, 2], P(('groups', 'dev')), parts along dimension 0, may hold values from 0 to 3, all different within a row; in each aligned block of 16 rows (0 to 15, 16 to 31, ...) at most 10 rows name the same one
- gate_weights: float32 [128, 2], P(('groups', 'dev')), parts along dimension 0, may hold values from 0.15 to 0.85, as said below
- w_gate: bfloat16 [3072, 65536], P(None, ('dev', 'cuts')), may hold values from -0.109375 to 0.109375
- w_up: bfloat16 [3072, 65536], P(None, ('dev', 'cuts')), may hold values from -0.109375 to 0.109375
- w_down: bfloat16 [65536, 3072], P(('dev', 'cuts')), may hold values from -0.046875 to 0.046875
Outputs:
- layer_out: bfloat16 [128, 3072], P(('groups', 'dev'), 'cuts'), parts along dimension 0
There are 2 independent parts, one for each index of `groups`. A program takes and returns all parts, laid end to end along the dimension named above; an argument that names none is the same for every part. Nothing has to cross between parts.
Inputs may be any that keep to these rules, and one draw needn't show every extreme that they name: `expert_ids`: the two experts of a row differ. Among the rows of one index of dev no expert is named by more than 10 rows, and in every draw some expert is named by exactly 10 rows of some index of dev. `lengths`: some row holds all 32 positions. `gate_weights`: the two weights of a row are positive and sum to one.
All inputs are finite; a program needn't handle non-finite values.
Results may differ from a plain program's by a relative error of at most 0.004.
Values may be sent and summed in bfloat16 or wider, within the bound.
A program may use at most 192 MiB of HBM per device.

v0:
```python
import math

import jax
import jax.numpy as jnp
from jax import lax
from jax.sharding import PartitionSpec as P

HD = 128
D = 3072
EXPERTS = 4
CAP = 10


def shards(
    residual,
    queries,
    keys,
    values,
    lengths,
    norm_gain,
    expert_ids,
    gate_weights,
    w_gate,
    w_up,
    w_down,
):
    row_count = residual.shape[0]
    dev_count = lax.axis_size("dev")
    group_size = dev_count // EXPERTS
    query_heads = queries.shape[1] // HD
    kv_local = keys.shape[2] // HD
    per_group = query_heads // kv_local
    context = keys.shape[1]
    query_view = queries.reshape(row_count, kv_local, per_group, HD)
    key_view = keys.reshape(row_count, context, kv_local, HD)
    value_view = values.reshape(row_count, context, kv_local, HD)
    scores = jnp.einsum(
        "rkgd,rtkd->rkgt", query_view, key_view, preferred_element_type=jnp.float32
    ) / math.sqrt(HD)
    visible = (jnp.arange(context, dtype=jnp.int32)[None, :] < lengths[:, None])[:, None, None, :]
    scores = jnp.where(visible, scores, -1e30)
    largest = jnp.max(scores, axis=-1, keepdims=True)
    weights = jnp.where(visible, jnp.exp(scores - largest), 0.0)
    probs = (weights / jnp.sum(weights, axis=-1, keepdims=True)).astype(jnp.bfloat16)
    attended = jnp.einsum("rkgt,rtkd->rkgd", probs, value_view, preferred_element_type=jnp.float32)
    mixed = residual.astype(jnp.float32) + attended.reshape(row_count, query_heads * HD)
    square_sum = lax.psum(jnp.sum(mixed * mixed, axis=1), "cuts")
    normed = (mixed * lax.rsqrt(square_sum / D + 1e-05)[:, None] * norm_gain).astype(jnp.bfloat16)
    members = expert_ids[:, :, None] == jnp.arange(EXPERTS, dtype=jnp.int32)[None, None, :]
    routed = jnp.any(members, axis=1).astype(jnp.int32)
    chosen = jnp.sum(members.astype(jnp.float32) * gate_weights[:, :, None], axis=1)
    slot_rank = jnp.cumsum(routed, axis=0) - 1
    placed = (routed[None, :, :] == 1) & (
        slot_rank[None, :, :] == jnp.arange(CAP, dtype=jnp.int32)[:, None, None]
    )
    selector = placed.transpose(2, 0, 1)
    selector_half = selector.astype(jnp.bfloat16)
    slot_total = dev_count * CAP
    whole = lax.all_gather(normed, "cuts", axis=1, tiled=True)
    boxed = jnp.einsum(
        "ecr,rd->ecd", selector_half, whole, preferred_element_type=jnp.float32
    ).astype(jnp.bfloat16)
    arrived = lax.all_to_all(
        jnp.repeat(boxed, group_size, axis=0), "dev", split_axis=0, concat_axis=0, tiled=True
    )
    flat = arrived.reshape(slot_total, arrived.shape[2])
    gate = jnp.dot(flat, w_gate, preferred_element_type=jnp.float32)
    upper = jnp.dot(flat, w_up, preferred_element_type=jnp.float32)
    hidden = (jax.nn.silu(gate) * upper).astype(jnp.bfloat16)
    partial_half = jnp.dot(hidden, w_down, preferred_element_type=jnp.float32).astype(jnp.bfloat16)
    weighted = selector.astype(jnp.float32) * chosen.T[:, None, :]
    rounded = lax.optimization_barrier(partial_half).astype(jnp.float32)
    share = lax.psum_scatter(
        rounded.astype(jnp.bfloat16), "cuts", scatter_dimension=1, tiled=True
    ).astype(jnp.float32)
    sent_back = lax.all_to_all(
        share.reshape(dev_count, CAP, share.shape[1]).astype(jnp.bfloat16),
        "dev",
        split_axis=0,
        concat_axis=0,
        tiled=True,
    ).astype(jnp.float32)
    per_expert = jnp.sum(sent_back.reshape(EXPERTS, group_size, CAP, share.shape[1]), axis=1)
    moe = jnp.einsum("ecr,ecd->rd", weighted, per_expert, precision=lax.Precision.HIGHEST)
    return (mixed + moe).astype(jnp.bfloat16)


def solution(mesh):
    placed = (
        P(("groups", "dev"), "cuts"),
        P(("groups", "dev"), "cuts"),
        P(("groups", "dev"), None, "cuts"),
        P(("groups", "dev"), None, "cuts"),
        P(("groups", "dev")),
        P("cuts"),
        P(("groups", "dev"), None),
        P(("groups", "dev"), None),
        P(None, ("dev", "cuts")),
        P(None, ("dev", "cuts")),
        P(("dev", "cuts"), None),
    )
    return jax.shard_map(
        shards, mesh=mesh, in_specs=placed, out_specs=P(("groups", "dev"), "cuts"), check_vma=False
    )
```

profile of v0, /device:TPU:0, one launch (start us, length us, event | category | flops | bytes accessed | tf_op | source)
XLA Modules:
  0.0 112.2 jit_solution(16959894715010823619)
XLA Ops:
  6.5 0.0 copy-start
  6.5 0.0 reduce-scatter.2.cloned.1.call-start
  6.5 0.8 reshape.82
  7.4 0.7 iota_compare_fusion.1
  8.1 1.2 %fusion.30 = (f32[16,6]{1,0:T(8,128)S(1)}, f32[16,6,32]{2,1,0:T(8,128)S(1)}) fusion(pred[16,32]{1,0:T(8,128)(4,1)S(1)} %iota_compare_fusion.1, bf16[16,6,128]{2,1,0:T(8,128)(2,1)S(1)} %reshape.82, bf16[16,32,128]{2,1,0:T(8,128)(2,1)} %param.13), kind=kOutput, calls=%fused_computation.44 | convolution fusion | flops 801823 | bytes 168832 | tf_op jit(solution)/shard_map/sub | solution.py:43
  9.3 0.0 copy-done
  9.3 0.2 fusion.15
  9.6 0.9 multiply_reduce_fusion
  10.4 8.3 %psum.7 = f32[16]{0:T(128)S(1)} all-reduce(f32[16]{0:T(128)S(1)} %multiply_reduce_fusion), channel_id=1, replica_groups=mesh['groups'=2,'dev'=4,'cuts'=4] {'cuts'}, use_global_device_ids=true, to_apply=%region_6.7 | all-reduce | flops 16 | bytes 128 | tf_op jit(solution)/shard_map/psum | solution.py:47
  18.8 0.8 multiply_convert_fusion
  19.6 5.3 %all_gather.3 = bf16[16,3072]{1,0:T(8,128)(2,1)S(1)} all-gather(bf16[16,768]{1,0:T(8,128)(2,1)S(1)} %multiply_convert_fusion), channel_id=1, replica_groups=mesh['groups'=2,'dev'=4,'cuts'=4] {'cuts'}, dimensions={1}, use_global_device_ids=true | all-gather | bytes 122880 | tf_op jit(solution)/shard_map/all_gather | solution.py:59
  24.9 0.7 fusion.27
  25.6 0.1 copy.22
  25.8 0.1 copy.23
  25.8 0.4 convolution_convert_fusion
  26.2 16.9 %all_to_all.10 = bf16[4,10,3072]{2,1,0:T(8,128)(2,1)S(1)} all-to-all(bf16[4,10,3072]{2,1,0:T(8,128)(2,1)S(1)} %convolution_convert_fusion), channel_id=1, replica_groups=mesh['groups'=2,'dev'=4,'cuts'=4] {'dev'}, dimensions={0} | all-to-all | bytes 491520 | tf_op jit(solution)/shard_map/all_to_all | solution.py:63
  43.1 0.1 reshape.84
  43.2 10.4 %fusion.31 = f32[40,4096]{1,0:T(8,128)S(1)} fusion(bf16[40,3072]{1,0:T(8,128)(2,1)S(1)} %reshape.84, bf16[3072,4096]{1,0:T(8,128)(2,1)} %param.19), kind=kOutput, calls=%fused_computation.45 | convolution fusion | flops 1006632960 | bytes 26066944 | tf_op jit(solution)/shard_map/dot_general | solution.py:67
  53.6 0.0 copy-start.2
  53.6 0.0 copy-start.3
  53.6 0.0 copy-start.1
  53.7 20.5 %convolution_convert_fusion.1 = bf16[40,3072]{1,0:T(8,128)(2,1)} fusion(bf16[4096,3072]{1,0:T(8,128)(2,1)} %param.21, bf16[40,3072]{1,0:T(8,128)(2,1)S(1)} %reshape.84, bf16[3072,4096]{1,0:T(8,128)(2,1)} %param.20, f32[40,4096]{1,0:T(8,128)S(1)} %fusion.31), kind=kOutput, calls=%fused_computation.4 | convolution fusion | flops 2014371840 | bytes 51478528 | tf_op jit(solution)/shard_map/dot_general | solution.py:70
  74.2 0.0 reduce-scatter.2.cloned.1.call-update
  74.2 18.3 %reduce-scatter.2.cloned.1.call-done = bf16[40,768]{1,0:T(8,128)(2,1)} async-done(((bf16[40,3072]{1,0:T(8,128)(2,1)}), bf16[40,768]{1,0:T(8,128)(2,1)}) %reduce-scatter.2.cloned.1.call-update) | async-done | bytes 61456 | tf_op jit(solution)/shard_map/reduce_scatter | solution.py:73
  92.5 1.5 %convert_element_type.53 = bf16[4,10,768]{2,1,0:T(8,128)(2,1)} reshape(bf16[40,768]{1,0:T(8,128)(2,1)} %reduce-scatter.2.cloned.1.call-done) | data formatting | bytes 122880 | tf_op jit(solution)/shard_map/convert_element_type | solution.py:77
  94.0 4.6 %all-to-all-start.1 = ((bf16[4,10,768]{2,1,0:T(8,128)(2,1)}), bf16[4,10,768]{2,1,0:T(8,128)(2,1)S(1)}, u32[]{:S(2)}, u32[]{:S(2)}) async-start(bf16[4,10,768]{2,1,0:T(8,128)(2,1)} %convert_element_type.53), calls=%async_computation.2 | async-start | bytes 196608 | tf_op jit(solution)/shard_map/all_to_all | solution.py:76
  98.6 0.0 copy-done.2
  98.6 0.0 copy-done.3
  98.6 5.8 %all-to-all-done.1 = bf16[4,10,768]{2,1,0:T(8,128)(2,1)S(1)} async-done(((bf16[4,10,768]{2,1,0:T(8,128)(2,1)}), bf16[4,10,768]{2,1,0:T(8,128)(2,1)S(1)}, u32[]{:S(2)}, u32[]{:S(2)}) %all-to-all-start.1) | async-done | bytes 61472 | tf_op jit(solution)/shard_map/all_to_all | solution.py:76
  104.4 0.0 copy-done.1
  104.4 1.0 fusion.7
  (5 shorter events, 0.1 us)
Async XLA Ops:
  6.5 2.8 %copy-start = (bf16[16,32,128]{2,1,0:T(8,128)(2,1)S(1)}, bf16[16,32,128]{2,1,0:T(8,128)(2,1)}, u32[]{:S(2)}) copy-start(bf16[16,32,128]{2,1,0:T(8,128)(2,1)} %param.14) | copy-start | bytes 393220
  6.5 85.9 %reduce-scatter.2.cloned.1.call-start = ((), (), s32[]{:S(2)}) async-start(), calls=%async_computation.3 | async-start | bytes 307200 | tf_op jit(solution)/shard_map/reduce_scatter | solution.py:73
  53.6 44.9 %copy-start.2 = (s32[16,2]{0,1:T(2,128)S(1)}, s32[16,2]{0,1:T(2,128)}, u32[]{:S(2)}) copy-start(s32[16,2]{0,1:T(2,128)} %param.17) | copy-start | bytes 388
  53.6 44.9 %copy-start.3 = (f32[16,2]{0,1:T(2,128)S(1)}, f32[16,2]{0,1:T(2,128)}, u32[]{:S(2)}) copy-start(f32[16,2]{0,1:T(2,128)} %param.18) | copy-start | bytes 388
  53.6 50.8 %copy-start.1 = (bf16[16,768]{1,0:T(8,128)(2,1)S(1)}, bf16[16,768]{1,0:T(8,128)(2,1)}, u32[]{:S(2)}) copy-start(bf16[16,768]{1,0:T(8,128)(2,1)} %param.11) | copy-start | bytes 73732
  94.0 10.4 %all-to-all-start.1 = ((bf16[4,10,768]{2,1,0:T(8,128)(2,1)}), bf16[4,10,768]{2,1,0:T(8,128)(2,1)S(1)}, u32[]{:S(2)}, u32[]{:S(2)}) async-start(bf16[4,10,768]{2,1,0:T(8,128)(2,1)} %convert_element_type.53), calls=%async_computation.2 | async-start | bytes 196608 | tf_op jit(solution)/shard_map/all_to_all | solution.py:76
Sparse Core Ops, SparseCore 0:
  74.3 18.1 reduce-scatter.1
where the time goes:
time: 113 us; the launch traced here: 112 us
  matrix products  33.7 us (30%)
  blocking collectives  30.5 us (27%)
  waiting for transfers between devices  24.1 us (21%)
  between operations  13.5 us (12%)
  starting transfers between devices  4.61 us (4%)
  other arithmetic  3.2 us (3%)
  local copies, waits for them, and re-layouts  2.58 us (2%)
    dot_general x1, matrix products, shards(): jnp.dot(hidden, w_down, preferred_element_type=jnp.float32)  20.5 us
    reduce_scatter x1, waiting for transfers between devices, shards(): lax.psum_scatter(rounded.astype(jnp.bfloat16), 'cuts', scatter_dimension=...  18.3 us
    all_to_all x1, blocking collectives, shards(): lax.all_to_all(jnp.repeat(boxed, group_size, axis=0), 'dev', split_axis=0...  16.9 us
    dot_general x1, matrix products, shards(): gate = jnp.dot(flat, w_gate, preferred_element_type=jnp.float32)  10.4 us
    psum x1, blocking collectives, shards(): square_sum = lax.psum(jnp.sum(mixed * mixed, axis=1), 'cuts')  8.34 us
    all_to_all x1, waiting for transfers between devices, shards(): lax.all_to_all(share.reshape(dev_count, CAP, share.shape[1]).astype(jnp.b...  5.81 us
    all_gather x1, blocking collectives, shards(): whole = lax.all_gather(normed, 'cuts', axis=1, tiled=True)  5.32 us
    all_to_all x1, starting transfers between devices, shards(): lax.all_to_all(share.reshape(dev_count, CAP, share.shape[1]).astype(jnp.b...  4.6 us
  transfers between devices with their start and end apart: 2, of which 2 were waited for; matrix products, arithmetic and copies ran while one was open for 0% of the time, Pallas kernels for 0%

commit v1 on v0

--- a/solution.py
+++ b/solution.py
@@ -1,17 +1,26 @@
+import functools
 import math
 
 import jax
 import jax.numpy as jnp
 from jax import lax
+from jax.experimental import pallas as pl
+from jax.experimental.pallas import tpu as pltpu
 from jax.sharding import PartitionSpec as P
 
 HD = 128
 D = 3072
 EXPERTS = 4
 CAP = 10
-
-
-def shards(
+MESH = pl.DeviceIdType.MESH
+
+UNIT = 1024
+WIDE = 512
+SLOTS = 56
+VMEM_BYTES = 64 * 1024 * 1024 - 256 * 1024
+
+
+def shards_general(
     residual,
     queries,
     keys,
@@ -85,6 +94,378 @@
     return (mixed + moe).astype(jnp.bfloat16)
 
 
+def layer_kernel(
+    nd,
+    nc,
+    res_hbm,
+    q_hbm,
+    k_hbm,
+    v_hbm,
+    meta_hbm,
+    gain_hbm,
+    wg_hbm,
+    wu_hbm,
+    wd_hbm,
+    out_ref,
+    res_v,
+    q_v,
+    k_v,
+    v_v,
+    meta_v,
+    gain_v,
+    ring,
+    xrecv,
+    xs,
+    scale_v,
+    hid,
+    mixed_v,
+    outbuf,
+    back,
+    small_sem,
+    ring_sem,
+    send1,
+    recv1,
+    send2,
+    recv2,
+    send3,
+    recv3,
+):
+    d = lax.axis_index("dev")
+    c = lax.axis_index("cuts")
+    rows = res_v.shape[0]
+    feat = res_v.shape[1]
+    heads = feat // HD
+    ctx = k_v.shape[1]
+    ff = wg_hbm.shape[2]
+    up_units = wg_hbm.shape[0]
+    down_units = wd_hbm.shape[0]
+    hid_chunks = ff // WIDE
+    half = WIDE // 2
+    subs = feat // half
+    down_chunks = (nc // 2) * subs
+
+    def peer(doff, coff):
+        return {"dev": lax.rem(d + doff, nd), "cuts": lax.rem(c + coff, nc)}
+
+    others = [(i, j) for i in range(nd) for j in range(nc) if (i, j) != (0, 0)]
+    barrier = pltpu.get_barrier_semaphore()
+    for doff, coff in others:
+        pl.semaphore_signal(barrier, inc=1, device_id=peer(doff, coff), device_id_type=MESH)
+
+    small = [
+        pltpu.make_async_copy(src, dst, small_sem.at[i])
+        for i, (src, dst) in enumerate(
+            [
+                (q_hbm, q_v),
+                (k_hbm, k_v),
+                (meta_hbm, meta_v),
+                (v_hbm, v_v),
+                (res_hbm, res_v),
+                (gain_hbm, gain_v),
+            ]
+        )
+    ]
+    for copy in small:
+        copy.start()
+
+    def up_copies(hc):
+        base = 2 * up_units * hc
+        return [
+            pltpu.make_async_copy(
+                src.at[:, :, pl.ds(pl.multiple_of(hc * WIDE, WIDE), WIDE)],
+                ring.at[pl.ds(base + i * up_units, up_units)],
+                ring_sem.at[2 * hc + i],
+            )
+            for i, src in enumerate((wg_hbm, wu_hbm))
+        ]
+
+    def down_slot(k):
+        unit = 2 * up_units * hid_chunks + down_units * k
+        return unit % SLOTS
+
+    def down_owner(k, side):
+        return lax.rem(c + 2 * (k % (nc // 2)) + side, nc)
+
+    def down_copies(k):
+        base = down_slot(k)
+        copies = []
+        for side in range(2):
+            at = down_owner(k, side) * feat + (k // (nc // 2)) * half
+            copies.append(
+                pltpu.make_async_copy(
+                    wd_hbm.at[:, :, pl.ds(pl.multiple_of(at, half), half)],
+                    ring.at[pl.ds(base, down_units), :, pl.ds(side * half, half)],
+                    ring_sem.at[2 * hid_chunks + 2 * k + side],
+                )
+            )
+        return copies
+
+    def start_up(hc, carry):
+        for copy in up_copies(hc):
+            copy.start()
+        return carry
+
+    lax.fori_loop(0, hid_chunks, start_up, 0)
+    ahead = 0
+    while ahead < down_chunks and 2 * up_units * hid_chunks + down_units * (ahead + 1) <= SLOTS:
+        for copy in down_copies(ahead):
+            copy.start()
+        ahead += 1
+
+    small[0].wait()
+    small[1].wait()
+    small[2].wait()
+    queries = jnp.concatenate([q_v[:, h * HD : (h + 1) * HD] for h in range(heads)], axis=0)
+    all_keys = k_v[...].reshape(rows * ctx, HD)
+    scores = lax.dot_general(
+        queries, all_keys, (((1,), (1,)), ((), ())), preferred_element_type=jnp.float32
+    ) * (1.0 / math.sqrt(HD))
+    meta = meta_v[...]
+    position = lax.broadcasted_iota(jnp.int32, (rows, rows * ctx), 1)
+    start = lax.broadcasted_iota(jnp.int32, (rows, rows * ctx), 0) * ctx
+    length = meta[:, EXPERTS : EXPERTS + 1].astype(jnp.int32)
+    visible = (position >= start) & (position < start + length)
+    probs = []
+    for h in range(heads):
+        mine = jnp.where(visible, scores[h * rows : (h + 1) * rows], -1e30)
+        largest = jnp.max(mine, axis=-1, keepdims=True)
+        weights = jnp.where(visible, jnp.exp(mine - largest), 0.0)
+        probs.append((weights / jnp.sum(weights, axis=-1, keepdims=True)).astype(jnp.bfloat16))
+    small[3].wait()
+    all_values = v_v[...].reshape(rows * ctx, HD)
+    attended = jnp.dot(
+        jnp.concatenate(probs, axis=0), all_values, preferred_element_type=jnp.float32
+    )
+    small[4].wait()
+    small[5].wait()
+    mixed = res_v[...].astype(jnp.float32) + jnp.concatenate(
+        [attended[h * rows : (h + 1) * rows] for h in range(heads)], axis=1
+    )
+    mixed_v[...] = mixed
+    squares = jnp.sum(mixed * mixed, axis=1, keepdims=True)
+    high = squares.astype(jnp.bfloat16).astype(jnp.float32)
+    lane = lax.broadcasted_iota(jnp.int32, (rows, HD), 1)
+    parts = jnp.where(lane < HD // 2, high, squares - high)
+    xrecv[d, c, :, pl.ds(0, feat)] = (mixed * gain_v[...]).astype(jnp.bfloat16)
+    xrecv[d, c, :, pl.ds(feat, HD)] = parts.astype(jnp.bfloat16)
+
+    pl.semaphore_wait(barrier, len(others))
+
+    def along_dev(doff):
+        return pltpu.make_async_remote_copy(
+            src_ref=xrecv.at[d, c],
+            dst_ref=xrecv.at[d, c],
+            send_sem=send1.at[doff - 1],
+            recv_sem=recv1.at[doff - 1],
+            device_id=peer(doff, 0),
+            device_id_type=MESH,
+        )
+
+    def along_cuts(doff, coff):
+        block = xrecv.at[lax.rem(d + nd - doff, nd), c]
+        return pltpu.make_async_remote_copy(
+            src_ref=block,
+            dst_ref=block,
+            send_sem=send2.at[coff - 1, doff],
+            recv_sem=recv2.at[coff - 1, doff],
+            device_id=peer(0, coff),
+            device_id_type=MESH,
+        )
+
+    for doff in range(1, nd):
+        along_dev(doff).start()
+    for coff in range(1, nc):
+        along_cuts(0, coff).start()
+    for doff in range(1, nd):
+        along_dev(doff).wait_recv()
+        for coff in range(1, nc):
+            along_cuts(doff, coff).start()
+    for doff in range(nd):
+        for coff in range(1, nc):
+            along_cuts(doff, coff).wait_recv()
+
+    for dd in range(nd):
+        total = jnp.zeros((rows, HD), jnp.float32)
+        for cc in range(nc):
+            xs[dd * rows : (dd + 1) * rows, cc * feat : (cc + 1) * feat] = xrecv[dd, cc, :, :feat]
+            total += xrecv[dd, cc, :, feat:].astype(jnp.float32)
+        square_sum = jnp.sum(total, axis=1, keepdims=True) * (2.0 / HD)
+        scale_v[dd * rows : (dd + 1) * rows, :] = jnp.broadcast_to(
+            lax.rsqrt(square_sum / (nc * feat) + 1e-05), (rows, HD)
+        )
+
+    def up_step(hc, carry):
+        for copy in up_copies(hc):
+            copy.wait()
+        base = 2 * up_units * hc
+        scale = scale_v[:, :1]
+        x = xs[...]
+        gate = jnp.dot(
+            x,
+            ring[pl.ds(base, up_units)].reshape(up_units * UNIT, WIDE),
+            preferred_element_type=jnp.float32,
+        )
+        upper = jnp.dot(
+            x,
+            ring[pl.ds(base + up_units, up_units)].reshape(up_units * UNIT, WIDE),
+            preferred_element_type=jnp.float32,
+        )
+        gate = gate * scale
+        upper = upper * scale
+        hid[:, pl.ds(pl.multiple_of(hc * WIDE, WIDE), WIDE)] = (
+            gate / (1.0 + jnp.exp(-gate)) * upper
+        ).astype(jnp.bfloat16)
+        return carry
+
+    done = 0
+    for k in range(ahead, down_chunks):
+        need = -(-(down_slot(k) + down_units) // (2 * up_units))
+        if need > done:
+            lax.fori_loop(done, need, up_step, 0)
+            done = need
+        for copy in down_copies(k):
+            copy.start()
+    lax.fori_loop(done, hid_chunks, up_step, 0)
+
+    def back_copies(k, side):
+        coff = 2 * (k % (nc // 2)) + side
+        at = (k // (nc // 2)) * half
+        copies = []
+        for doff in range(nd):
+            src = outbuf.at[k, side, lax.rem(d + doff, nd)]
+            dst = back.at[k // (nc // 2), d * nc + c]
+            if doff == 0 and coff == 0:
+                copies.append(pltpu.make_async_copy(src, dst, recv3.at[k // (nc // 2)]))
+            else:
+                copies.append(
+                    pltpu.make_async_remote_copy(
+                        src_ref=src,
+                        dst_ref=dst,
+                        send_sem=send3.at[k, side, doff],
+                        recv_sem=recv3.at[k // (nc // 2)],
+                        device_id=peer(doff, coff),
+                        device_id_type=MESH,
+                    )
+                )
+        return copies
+
+    for k in range(down_chunks):
+        for copy in down_copies(k):
+            copy.wait()
+        acc = jnp.dot(
+            hid[...],
+            ring[pl.ds(down_slot(k), down_units)].reshape(down_units * UNIT, WIDE),
+            preferred_element_type=jnp.float32,
+        ).astype(jnp.bfloat16)
+        for side in range(2):
+            outbuf[k, side] = acc[:, side * half : (side + 1) * half].reshape(nd, rows, half)
+            for copy in back_copies(k, side):
+                copy.start()
+
+    for sub in range(subs):
+        pltpu.make_async_copy(back.at[sub], back.at[sub], recv3.at[sub]).wait()
+        total = mixed_v[:, sub * half : (sub + 1) * half]
+        for dd in range(nd):
+            part = back[sub, dd * nc].astype(jnp.float32)
+            for cc in range(1, nc):
+                part += back[sub, dd * nc + cc].astype(jnp.float32)
+            total += meta[:, dd : dd + 1] * part
+        out_ref[:, sub * half : (sub + 1) * half] = total.astype(out_ref.dtype)
+
+    for doff in range(1, nd):
+        along_dev(doff).wait_send()
+    for doff in range(nd):
+        for coff in range(1, nc):
+            along_cuts(doff, coff).wait_send()
+    for k in range(down_chunks):
+        for side in range(2):
+            for doff, copy in enumerate(back_copies(k, side)):
+                if doff != 0 or 2 * (k % (nc // 2)) + side != 0:
+                    copy.wait_send()
+
+
+def shards_fused(
+    residual,
+    queries,
+    keys,
+    values,
+    lengths,
+    norm_gain,
+    expert_ids,
+    gate_weights,
+    w_gate,
+    w_up,
+    w_down,
+):
+    nd, nc = lax.axis_size("dev"), lax.axis_size("cuts")
+    rows, feat = residual.shape
+    ctx = keys.shape[1]
+    ff = w_gate.shape[1]
+    half = WIDE // 2
+    subs = feat // half
+    hid_chunks = ff // WIDE
+    down_chunks = (nc // 2) * subs
+    up_units, down_units = D // UNIT, ff // UNIT
+    lane = jnp.arange(HD, dtype=jnp.int32)[None, :]
+    chosen = sum(
+        jnp.where(expert_ids[:, i : i + 1] == lane, gate_weights[:, i : i + 1], 0.0)
+        for i in range(expert_ids.shape[1])
+    )
+    meta = jnp.where(lane == EXPERTS, lengths[:, None].astype(jnp.float32), chosen)
+    bf16, f32 = jnp.bfloat16, jnp.float32
+    total = nd * rows
+    return pl.pallas_call(
+        functools.partial(layer_kernel, nd, nc),
+        out_shape=jax.ShapeDtypeStruct((rows, feat), bf16),
+        in_specs=[pl.BlockSpec(memory_space=pl.ANY)] * 9,
+        out_specs=pl.BlockSpec(memory_space=pltpu.VMEM),
+        scratch_shapes=[
+            pltpu.VMEM((rows, feat), bf16),
+            pltpu.VMEM((rows, feat), bf16),
+            pltpu.VMEM((rows, ctx, HD), bf16),
+            pltpu.VMEM((rows, ctx, HD), bf16),
+            pltpu.VMEM((rows, HD), f32),
+            pltpu.VMEM((1, feat), f32),
+            pltpu.VMEM((SLOTS, UNIT, WIDE), bf16),
+            pltpu.VMEM((nd, nc, rows, feat + HD), bf16),
+            pltpu.VMEM((total, D), bf16),
+            pltpu.VMEM((total, HD), f32),
+            pltpu.VMEM((total, ff), bf16),
+            pltpu.VMEM((rows, feat), f32),
+            pltpu.VMEM((down_chunks, 2, nd, rows, half), bf16),
+            pltpu.VMEM((subs, nd * nc, rows, half), bf16),
+            pltpu.SemaphoreType.DMA((6,)),
+            pltpu.SemaphoreType.DMA((2 * hid_chunks + 2 * down_chunks,)),
+            pltpu.SemaphoreType.DMA((nd - 1,)),
+            pltpu.SemaphoreType.DMA((nd - 1,)),
+            pltpu.SemaphoreType.DMA((nc - 1, nd)),
+            pltpu.SemaphoreType.DMA((nc - 1, nd)),
+            pltpu.SemaphoreType.DMA((down_chunks, 2, nd)),
+            pltpu.SemaphoreType.DMA((subs,)),
+        ],
+        compiler_params=pltpu.CompilerParams(
+            collective_id=0, has_side_effects=True, vmem_limit_bytes=VMEM_BYTES
+        ),
+        cost_estimate=pl.CostEstimate(
+            flops=6 * total * D * ff, bytes_accessed=6 * D * ff, transcendentals=total * ff
+        ),
+    )(
+        residual,
+        queries,
+        keys,
+        values,
+        meta,
+        norm_gain.reshape(1, feat),
+        w_gate.reshape(up_units, UNIT, ff),
+        w_up.reshape(up_units, UNIT, ff),
+        w_down.reshape(down_units, UNIT, D),
+    )
+
+
+def fits(mesh):
+    return mesh.shape["dev"] == EXPERTS and mesh.shape["cuts"] == 4
+
+
 def solution(mesh):
     placed = (
         P(("groups", "dev"), "cuts"),
@@ -100,5 +481,9 @@
         P(("dev", "cuts"), None),
     )
     return jax.shard_map(
-        shards, mesh=mesh, in_specs=placed, out_specs=P(("groups", "dev"), "cuts"), check_vma=False
-    )
+        shards_fused if fits(mesh) else shards_general,
+        mesh=mesh,
+        in_specs=placed,
+        out_specs=P(("groups", "dev"), "cuts"),
+        check_vma=False,
+    )

time: 113 us -> 42.8 us (0.38)
  Pallas kernels: 0 us -> 37 us
  matrix products: 33.7 us -> 0 us
  blocking collectives: 30.5 us -> 0 us
  waiting for transfers between devices: 24.1 us -> 0 us
  between operations: 13.5 us -> 0.01 us
  starting transfers between devices: 4.61 us -> 0 us
  other arithmetic: 3.2 us -> 1.34 us
  local copies, waits for them, and re-layouts: 2.58 us -> 4.14 us
    pallas_call x0 -> x1, Pallas kernels: none -> 37 us  [shards_fused(): pl.pallas_call(functools.partial(layer_kernel, nd, nc), out_shape=jax.Sha...]
    dot_general x5 -> x0, matrix products: 32.5 us -> none  [the longest x1 20.5 us: shards(): jnp.dot(hidden, w_down, preferred_element_type=jnp.float32)]
    reduce_scatter x1 -> x0, waiting for transfers between devices: 18.3 us -> none  [shards(): lax.psum_scatter(rounded.astype(jnp.bfloat16), 'cuts', scatter_dimension=...]
    all_to_all x1 -> x0, blocking collectives: 16.9 us -> none  [shards(): lax.all_to_all(jnp.repeat(boxed, group_size, axis=0), 'dev', split_axis=0...]
    psum x1 -> x0, blocking collectives: 8.34 us -> none  [shards(): square_sum = lax.psum(jnp.sum(mixed * mixed, axis=1), 'cuts')]
    all_to_all x1 -> x0, waiting for transfers between devices: 5.81 us -> none  [shards(): lax.all_to_all(share.reshape(dev_count, CAP, share.shape[1]).astype(jnp.b...]
    all_gather x1 -> x0, blocking collectives: 5.32 us -> none  [shards(): whole = lax.all_gather(normed, 'cuts', axis=1, tiled=True)]
    all_to_all x1 -> x0, starting transfers between devices: 4.6 us -> none  [shards(): lax.all_to_all(share.reshape(dev_count, CAP, share.shape[1]).astype(jnp.b...]
  transfers between devices with their start and end apart: 2 -> 0, of which waited for: 2 -> 0; matrix products, arithmetic and copies ran while one was open for 0% -> 0% of each run, Pallas kernels for 0% -> 0%
where the time goes in v1:
time: 42.8 us; the launch traced here: 42.5 us
  Pallas kernels  37 us (86%)
  local copies, waits for them, and re-layouts  4.14 us (10%)
  other arithmetic  1.34 us (3%)
    pallas_call x1, Pallas kernels, shards_fused(): pl.pallas_call(functools.partial(layer_kernel, nd, nc), out_shape=jax.Sha...  37 us
    unnamed x1, local copies, waits for them, and re-layouts  1.35 us
    reshape x1, local copies, waits for them, and re-layouts, shards_fused(): norm_gain.reshape(1, feat)  1.28 us

profile of v1, /device:TPU:0, one launch (start us, length us, event | category | flops | bytes accessed | tf_op | source)
XLA Modules:
  0.0 42.5 jit_solution(9971452789874778010)
XLA Ops:
  0.0 0.7 %convert_element_type.4 = f32[16]{0:T(128)S(1)} convert(s32[16]{0:T(128)} %param.15) | non-fusion elementwise | flops 16 | bytes 128 | tf_op jit(solution)/shard_map/convert_element_type | solution.py:414
  0.7 0.8 %slice_bitcast_fusion.3 = (s32[16]{0:T(128)S(1)}, s32[16]{0:T(128)S(1)}) fusion(s32[16,2]{0,1:T(2,128)} %param.17), kind=kLoop, calls=%fused_computation.6 | loop fusion | bytes 256 | tf_op jit(solution)/shard_map/eq | solution.py:411
  1.4 0.8 %slice_bitcast_fusion.2 = (f32[16]{0:T(128)S(1)}, f32[16]{0:T(128)S(1)}) fusion(f32[16,2]{0,1:T(2,128)} %param.18), kind=kLoop, calls=%fused_computation.5 | loop fusion | bytes 256 | tf_op jit(solution)/shard_map/jit(_where)/broadcast_in_dim | solution.py:411
  2.2 1.3 %reshape.19.gain_hbm = f32[1,768]{1,0:T(1,128)} reshape(f32[768]{0:T(1024)} %param.16) | data formatting | bytes 6144 | tf_op jit(solution)/shard_map/reshape | solution.py:458
  3.5 0.7 %add_select_fusion.meta_hbm = f32[16,128]{1,0:T(8,128)} fusion(f32[16]{0:T(128)S(1)} %get-tuple-element.8, s32[16]{0:T(128)S(1)} %get-tuple-element.6, f32[16]{0:T(128)S(1)} %get-tuple-element.7, s32[16]{0:T(128)S(1)} %get-tuple-element.5, f32[16]{0:T(128)S(1)} %convert_element_type.4, pred[128]{0:T(512)(128)(4,1)S(1)} %iota_compare_fusion.2), kind=kLoop, calls=%fused_computation | loop fusion | flops 12288 | bytes 8640 | tf_op jit(solution)/shard_map/jit(_where)/select_n | solution.py:414
  4.1 37.0 %shard_map.109 = bf16[16,768]{1,0:T(8,128)(2,1)} custom-call(bf16[16,768]{1,0:T(8,128)(2,1)} %res_hbm.1, bf16[16,768]{1,0:T(8,128)(2,1)} %q_hbm.1, bf16[16,32,128]{2,1,0:T(8,128)(2,1)} %k_hbm.1, bf16[16,32,128]{2,1,0:T(8,128)(2,1)} %v_hbm.1, f32[16,128]{1,0:T(8,128)} %add_select_fusion.meta_hbm, f32[1,768]{1,0:T(1,128)} %reshape.19.gain_hbm, ...), custom_call_target="tpu_custom_call" | custom-call | flops 4831838208 | bytes 75497472 | tf_op jit(solution)/shard_map/pallas_call | solution.py:417
  41.2 1.3 %copy.13 = bf16[16,768]{1,0:T(8,128)(2,1)} copy(bf16[16,768]{1,0:T(8,128)(2,1)} %shard_map.109) | data formatting | bytes 49152
  (1 shorter events, 0.0 us)

commit v2 on v1

--- a/solution.py
+++ b/solution.py
@@ -101,8 +101,10 @@
     q_hbm,
     k_hbm,
     v_hbm,
-    meta_hbm,
+    len_hbm,
     gain_hbm,
+    ids_hbm,
+    gw_hbm,
     wg_hbm,
     wu_hbm,
     wd_hbm,
@@ -111,8 +113,11 @@
     q_v,
     k_v,
     v_v,
-    meta_v,
+    len_v,
     gain_v,
+    ids_v,
+    gw_v,
+    chosen_v,
     ring,
     xrecv,
     xs,
@@ -120,15 +125,19 @@
     hid,
     mixed_v,
     outbuf,
+    cutrecv,
+    summed,
     back,
     small_sem,
     ring_sem,
-    send1,
-    recv1,
-    send2,
-    recv2,
-    send3,
-    recv3,
+    dev_send,
+    dev_recv,
+    cut_send,
+    cut_recv,
+    part_send,
+    part_recv,
+    sum_send,
+    sum_recv,
 ):
     d = lax.axis_index("dev")
     c = lax.axis_index("cuts")
@@ -144,13 +153,23 @@
     subs = feat // half
     down_chunks = (nc // 2) * subs
 
-    def peer(doff, coff):
-        return {"dev": lax.rem(d + doff, nd), "cuts": lax.rem(c + coff, nc)}
-
-    others = [(i, j) for i in range(nd) for j in range(nc) if (i, j) != (0, 0)]
+    mate = c + 1 - 2 * (c % 2)
+
+    def cut_at(step):
+        near = c if step % 2 == 0 else mate
+        return lax.rem(near + (step // 2) * 2, nc)
+
+    def on_dev(doff):
+        return {"dev": lax.rem(d + doff, nd), "cuts": c}
+
+    def on_cut(step):
+        return {"dev": d, "cuts": cut_at(step)}
+
     barrier = pltpu.get_barrier_semaphore()
-    for doff, coff in others:
-        pl.semaphore_signal(barrier, inc=1, device_id=peer(doff, coff), device_id_type=MESH)
+    for doff in range(1, nd):
+        pl.semaphore_signal(barrier, inc=1, device_id=on_dev(doff), device_id_type=MESH)
+    for step in range(1, nc):
+        pl.semaphore_signal(barrier, inc=1, device_id=on_cut(step), device_id_type=MESH)
 
     small = [
         pltpu.make_async_copy(src, dst, small_sem.at[i])
@@ -158,10 +177,12 @@
             [
                 (q_hbm, q_v),
                 (k_hbm, k_v),
-                (meta_hbm, meta_v),
+                (len_hbm, len_v),
                 (v_hbm, v_v),
                 (res_hbm, res_v),
                 (gain_hbm, gain_v),
+                (ids_hbm, ids_v),
+                (gw_hbm, gw_v),
             ]
         )
     ]
@@ -184,13 +205,13 @@
         return unit % SLOTS
 
     def down_owner(k, side):
-        return lax.rem(c + 2 * (k % (nc // 2)) + side, nc)
+        return nc - 2 - 2 * (k % (nc // 2)) + side
 
     def down_copies(k):
         base = down_slot(k)
         copies = []
         for side in range(2):
-            at = down_owner(k, side) * feat + (k // (nc // 2)) * half
+            at = cut_at(down_owner(k, side)) * feat + (k // (nc // 2)) * half
             copies.append(
                 pltpu.make_async_copy(
                     wd_hbm.at[:, :, pl.ds(pl.multiple_of(at, half), half)],
@@ -220,10 +241,16 @@
     scores = lax.dot_general(
         queries, all_keys, (((1,), (1,)), ((), ())), preferred_element_type=jnp.float32
     ) * (1.0 / math.sqrt(HD))
-    meta = meta_v[...]
+    diagonal = lax.broadcasted_iota(jnp.int32, (rows, rows), 0) == lax.broadcasted_iota(
+        jnp.int32, (rows, rows), 1
+    )
+
+    def as_column(row):
+        return jnp.sum(jnp.where(diagonal, row, 0.0), axis=1, keepdims=True)
+
     position = lax.broadcasted_iota(jnp.int32, (rows, rows * ctx), 1)
     start = lax.broadcasted_iota(jnp.int32, (rows, rows * ctx), 0) * ctx
-    length = meta[:, EXPERTS : EXPERTS + 1].astype(jnp.int32)
+    length = as_column(len_v[...].reshape(1, rows).astype(jnp.float32)).astype(jnp.int32)
     visible = (position >= start) & (position < start + length)
     probs = []
     for h in range(heads):
@@ -246,43 +273,54 @@
     high = squares.astype(jnp.bfloat16).astype(jnp.float32)
     lane = lax.broadcasted_iota(jnp.int32, (rows, HD), 1)
     parts = jnp.where(lane < HD // 2, high, squares - high)
-    xrecv[d, c, :, pl.ds(0, feat)] = (mixed * gain_v[...]).astype(jnp.bfloat16)
+    xrecv[d, c, :, pl.ds(0, feat)] = (mixed * gain_v[...].reshape(1, feat)).astype(jnp.bfloat16)
     xrecv[d, c, :, pl.ds(feat, HD)] = parts.astype(jnp.bfloat16)
 
-    pl.semaphore_wait(barrier, len(others))
+    pl.semaphore_wait(barrier, nd + nc - 2)
 
     def along_dev(doff):
         return pltpu.make_async_remote_copy(
             src_ref=xrecv.at[d, c],
             dst_ref=xrecv.at[d, c],
-            send_sem=send1.at[doff - 1],
-            recv_sem=recv1.at[doff - 1],
-            device_id=peer(doff, 0),
+            send_sem=dev_send.at[doff - 1],
+            recv_sem=dev_recv.at[doff - 1],
+            device_id=on_dev(doff),
             device_id_type=MESH,
         )
 
-    def along_cuts(doff, coff):
-        block = xrecv.at[lax.rem(d + nd - doff, nd), c]
+    def along_cuts(doff, step):
+        block = xrecv.at[lax.rem(d + nd - doff, nd), c if step < 3 else cut_at(2)]
         return pltpu.make_async_remote_copy(
             src_ref=block,
             dst_ref=block,
-            send_sem=send2.at[coff - 1, doff],
-            recv_sem=recv2.at[coff - 1, doff],
-            device_id=peer(0, coff),
+            send_sem=cut_send.at[step - 1, doff],
+            recv_sem=cut_recv.at[step - 1, doff],
+            device_id=on_cut(2 if step == 2 else 1),
             device_id_type=MESH,
         )
 
     for doff in range(1, nd):
         along_dev(doff).start()
-    for coff in range(1, nc):
-        along_cuts(0, coff).start()
+    along_cuts(0, 2).start()
+    along_cuts(0, 1).start()
+    small[6].wait()
+    small[7].wait()
+    ids = ids_v[...]
+    gw = gw_v[...]
+    for e in range(EXPERTS):
+        named = jnp.sum(jnp.where(ids == e, gw, 0.0), axis=0, keepdims=True)
+        chosen_v[e] = jnp.broadcast_to(as_column(named), (rows, HD))
     for doff in range(1, nd):
         along_dev(doff).wait_recv()
-        for coff in range(1, nc):
-            along_cuts(doff, coff).start()
+        along_cuts(doff, 2).start()
+        along_cuts(doff, 1).start()
+        along_cuts(doff - 1, 2).wait_recv()
+        along_cuts(doff - 1, 3).start()
+    along_cuts(nd - 1, 2).wait_recv()
+    along_cuts(nd - 1, 3).start()
     for doff in range(nd):
-        for coff in range(1, nc):
-            along_cuts(doff, coff).wait_recv()
+        along_cuts(doff, 1).wait_recv()
+        along_cuts(doff, 3).wait_recv()
 
     for dd in range(nd):
         total = jnp.zeros((rows, HD), jnp.float32)
@@ -327,27 +365,41 @@
             copy.start()
     lax.fori_loop(done, hid_chunks, up_step, 0)
 
-    def back_copies(k, side):
-        coff = 2 * (k % (nc // 2)) + side
-        at = (k // (nc // 2)) * half
-        copies = []
-        for doff in range(nd):
-            src = outbuf.at[k, side, lax.rem(d + doff, nd)]
-            dst = back.at[k // (nc // 2), d * nc + c]
-            if doff == 0 and coff == 0:
-                copies.append(pltpu.make_async_copy(src, dst, recv3.at[k // (nc // 2)]))
-            else:
-                copies.append(
-                    pltpu.make_async_remote_copy(
-                        src_ref=src,
-                        dst_ref=dst,
-                        send_sem=send3.at[k, side, doff],
-                        recv_sem=recv3.at[k // (nc // 2)],
-                        device_id=peer(doff, coff),
-                        device_id_type=MESH,
-                    )
-                )
-        return copies
+    def part_copy(k, side):
+        step, sub = down_owner(k, side), k // (nc // 2)
+        return pltpu.make_async_remote_copy(
+            src_ref=outbuf.at[k, side],
+            dst_ref=cutrecv.at[sub, step - 1],
+            send_sem=part_send.at[sub, step - 1],
+            recv_sem=part_recv.at[sub, step - 1],
+            device_id=on_cut(step),
+            device_id_type=MESH,
+        )
+
+    def sum_copy(sub, doff):
+        return pltpu.make_async_remote_copy(
+            src_ref=summed.at[sub, lax.rem(d + doff, nd)],
+            dst_ref=back.at[sub, d],
+            send_sem=sum_send.at[sub, doff - 1],
+            recv_sem=sum_recv.at[sub, doff - 1],
+            device_id=on_dev(doff),
+            device_id_type=MESH,
+        )
+
+    def far_parts(k):
+        return [side for side in range(2) if down_owner(k, side) != 0]
+
+    def add_parts(sub):
+        last = sub * (nc // 2) + nc // 2 - 1
+        total = outbuf[last, 0].astype(jnp.float32)
+        for k in range(last + 1 - nc // 2, last + 1):
+            for side in far_parts(k):
+                part_copy(k, side).wait_recv()
+                total += cutrecv[sub, down_owner(k, side) - 1].astype(jnp.float32)
+        summed[sub] = total.astype(jnp.bfloat16).reshape(nd, rows, half)
+        for doff in range(1, nd):
+            sum_copy(sub, doff).start()
+        back[sub, d] = summed[sub, d]
 
     for k in range(down_chunks):
         for copy in down_copies(k):
@@ -358,30 +410,32 @@
             preferred_element_type=jnp.float32,
         ).astype(jnp.bfloat16)
         for side in range(2):
-            outbuf[k, side] = acc[:, side * half : (side + 1) * half].reshape(nd, rows, half)
-            for copy in back_copies(k, side):
-                copy.start()
+            outbuf[k, side] = acc[:, side * half : (side + 1) * half]
+        for side in far_parts(k):
+            part_copy(k, side).start()
+        if k >= nc // 2 and k % (nc // 2) == 0:
+            add_parts(k // (nc // 2) - 1)
+    add_parts(subs - 1)
 
     for sub in range(subs):
-        pltpu.make_async_copy(back.at[sub], back.at[sub], recv3.at[sub]).wait()
         total = mixed_v[:, sub * half : (sub + 1) * half]
+        for doff in range(1, nd):
+            sum_copy(sub, doff).wait_recv()
         for dd in range(nd):
-            part = back[sub, dd * nc].astype(jnp.float32)
-            for cc in range(1, nc):
-                part += back[sub, dd * nc + cc].astype(jnp.float32)
-            total += meta[:, dd : dd + 1] * part
-        out_ref[:, sub * half : (sub + 1) * half] = total.astype(out_ref.dtype)
+            total += chosen_v[dd, :, :1] * back[sub, dd].astype(jnp.float32)
+        out_ref[:, sub * half : (sub + 1) * half] = total
 
     for doff in range(1, nd):
         along_dev(doff).wait_send()
     for doff in range(nd):
-        for coff in range(1, nc):
-            along_cuts(doff, coff).wait_send()
+        for step in range(1, nc):
+            along_cuts(doff, step).wait_send()
     for k in range(down_chunks):
-        for side in range(2):
-            for doff, copy in enumerate(back_copies(k, side)):
-                if doff != 0 or 2 * (k % (nc // 2)) + side != 0:
-                    copy.wait_send()
+        for side in far_parts(k):
+            part_copy(k, side).wait_send()
+    for sub in range(subs):
+        for doff in range(1, nd):
+            sum_copy(sub, doff).wait_send()
 
 
 def shards_fused(
@@ -406,42 +460,43 @@
     hid_chunks = ff // WIDE
     down_chunks = (nc // 2) * subs
     up_units, down_units = D // UNIT, ff // UNIT
-    lane = jnp.arange(HD, dtype=jnp.int32)[None, :]
-    chosen = sum(
-        jnp.where(expert_ids[:, i : i + 1] == lane, gate_weights[:, i : i + 1], 0.0)
-        for i in range(expert_ids.shape[1])
-    )
-    meta = jnp.where(lane == EXPERTS, lengths[:, None].astype(jnp.float32), chosen)
     bf16, f32 = jnp.bfloat16, jnp.float32
     total = nd * rows
     return pl.pallas_call(
         functools.partial(layer_kernel, nd, nc),
-        out_shape=jax.ShapeDtypeStruct((rows, feat), bf16),
-        in_specs=[pl.BlockSpec(memory_space=pl.ANY)] * 9,
+        out_shape=jax.ShapeDtypeStruct((rows, feat), f32),
+        in_specs=[pl.BlockSpec(memory_space=pl.ANY)] * 11,
         out_specs=pl.BlockSpec(memory_space=pltpu.VMEM),
         scratch_shapes=[
             pltpu.VMEM((rows, feat), bf16),
             pltpu.VMEM((rows, feat), bf16),
             pltpu.VMEM((rows, ctx, HD), bf16),
             pltpu.VMEM((rows, ctx, HD), bf16),
-            pltpu.VMEM((rows, HD), f32),
-            pltpu.VMEM((1, feat), f32),
+            pltpu.VMEM((rows,), jnp.int32),
+            pltpu.VMEM((feat,), f32),
+            pltpu.VMEM(expert_ids.shape[::-1], jnp.int32),
+            pltpu.VMEM(expert_ids.shape[::-1], f32),
+            pltpu.VMEM((EXPERTS, rows, HD), f32),
             pltpu.VMEM((SLOTS, UNIT, WIDE), bf16),
             pltpu.VMEM((nd, nc, rows, feat + HD), bf16),
             pltpu.VMEM((total, D), bf16),
             pltpu.VMEM((total, HD), f32),
             pltpu.VMEM((total, ff), bf16),
             pltpu.VMEM((rows, feat), f32),
-            pltpu.VMEM((down_chunks, 2, nd, rows, half), bf16),
-            pltpu.VMEM((subs, nd * nc, rows, half), bf16),
-            pltpu.SemaphoreType.DMA((6,)),
+            pltpu.VMEM((down_chunks, 2, total, half), bf16),
+            pltpu.VMEM((subs, nc - 1, total, half), bf16),
+            pltpu.VMEM((subs, nd, rows, half), bf16),
+            pltpu.VMEM((subs, nd, rows, half), bf16),
+            pltpu.SemaphoreType.DMA((8,)),
             pltpu.SemaphoreType.DMA((2 * hid_chunks + 2 * down_chunks,)),
             pltpu.SemaphoreType.DMA((nd - 1,)),
             pltpu.SemaphoreType.DMA((nd - 1,)),
             pltpu.SemaphoreType.DMA((nc - 1, nd)),
             pltpu.SemaphoreType.DMA((nc - 1, nd)),
-            pltpu.SemaphoreType.DMA((down_chunks, 2, nd)),
-            pltpu.SemaphoreType.DMA((subs,)),
+            pltpu.SemaphoreType.DMA((subs, nc - 1)),
+            pltpu.SemaphoreType.DMA((subs, nc - 1)),
+            pltpu.SemaphoreType.DMA((subs, nd - 1)),
+            pltpu.SemaphoreType.DMA((subs, nd - 1)),
         ],
         compiler_params=pltpu.CompilerParams(
             collective_id=0, has_side_effects=True, vmem_limit_bytes=VMEM_BYTES
@@ -454,12 +509,14 @@
         queries,
         keys,
         values,
-        meta,
-        norm_gain.reshape(1, feat),
+        lengths,
+        norm_gain,
+        expert_ids.T,
+        gate_weights.T,
         w_gate.reshape(up_units, UNIT, ff),
         w_up.reshape(up_units, UNIT, ff),
         w_down.reshape(down_units, UNIT, D),
-    )
+    ).astype(bf16)
 
 
 def fits(mesh):

time: 42.8 us -> 39.5 us (0.923)
  local copies, waits for them, and re-layouts: 4.14 us -> 0 us
  Pallas kernels: 37 us -> 37.9 us
    unnamed x1 -> x0, local copies, waits for them, and re-layouts: 1.35 us -> none
    reshape x1 -> x0, local copies, waits for them, and re-layouts: 1.28 us -> none  [shards_fused(): norm_gain.reshape(1, feat)]
    pallas_call x1, Pallas kernels: 37 us -> 37.9 us  [shards_fused(): pl.pallas_call(functools.partial(layer_kernel, nd, nc), out_shape=jax.Sha...]
    broadcast_in_dim x1 -> x0, local copies, waits for them, and re-layouts: 0.76 us -> none  [shards_fused(): jnp.where(expert_ids[:, i:i + 1] == lane, gate_weights[:, i:i + 1], 0.0)]
    eq x1 -> x0, local copies, waits for them, and re-layouts: 0.76 us -> none  [shards_fused(): expert_ids[:, i:i + 1] == lane]
    convert_element_type x1, other arithmetic: 0.66 us -> 1.41 us  [shards_fused(): return pl.pallas_call(functools.partial(layer_kernel, nd, nc), out_shape=...]
    select_n x1 -> x0, other arithmetic: 0.67 us -> none  [shards_fused(): jnp.where(lane == EXPERTS, lengths[:, None].astype(jnp.float32), chosen)]
where the time goes in v2:
time: 39.5 us; the launch traced here: 39.3 us
  Pallas kernels  37.9 us (96%)
  other arithmetic  1.41 us (4%)
    pallas_call x1, Pallas kernels, shards_fused(): pl.pallas_call(functools.partial(layer_kernel, nd, nc), out_shape=jax.Sha...  37.9 us
    convert_element_type x1, other arithmetic, shards_fused(): return pl.pallas_call(functools.partial(layer_kernel, nd, nc), out_shape=...  1.41 us

profile of v2, /device:TPU:0, one launch (start us, length us, event | category | flops | bytes accessed | tf_op | source)
XLA Modules:
  0.0 39.3 jit_solution(13080271175576331840)
XLA Ops:
  0.0 37.9 %shard_map.109 = f32[16,768]{1,0:T(8,128)} custom-call(bf16[16,768]{1,0:T(8,128)(2,1)} %res_hbm.1, bf16[16,768]{1,0:T(8,128)(2,1)} %q_hbm.1, bf16[16,32,128]{2,1,0:T(8,128)(2,1)} %k_hbm.1, bf16[16,32,128]{2,1,0:T(8,128)(2,1)} %v_hbm.1, s32[16]{0:T(128)} %len_hbm.1, f32[768]{0:T(1024)} %gain_hbm.1, s32[2,16]{1,0:T(2,128)} %bitcast.8, f32[2,16]{1,0:T(2,128)} %bitcast.9, ...), custom_call_target="tpu_custom_call" | custom-call | flops 4831838208 | bytes 75497472 | tf_op jit(solution)/shard_map/pallas_call | solution.py:465
  37.9 1.4 %convert_element_type.3 = bf16[16,768]{1,0:T(8,128)(2,1)} convert(f32[16,768]{1,0:T(8,128)} %shard_map.109) | non-fusion elementwise | flops 12288 | bytes 73728 | tf_op jit(solution)/shard_map/convert_element_type | solution.py:519

commit v3 on v2

--- a/solution.py
+++ b/solution.py
@@ -14,9 +14,9 @@
 CAP = 10
 MESH = pl.DeviceIdType.MESH
 
-UNIT = 1024
+UNIT = 256
 WIDE = 512
-SLOTS = 56
+SLOTS = 224
 VMEM_BYTES = 64 * 1024 * 1024 - 256 * 1024
 
 
@@ -122,6 +122,8 @@
     xrecv,
     xs,
     scale_v,
+    gate_v,
+    upper_v,
     hid,
     mixed_v,
     outbuf,
@@ -147,6 +149,7 @@
     ctx = k_v.shape[1]
     ff = wg_hbm.shape[2]
     up_units = wg_hbm.shape[0]
+    feat_units = feat // UNIT
     down_units = wd_hbm.shape[0]
     hid_chunks = ff // WIDE
     half = WIDE // 2
@@ -189,13 +192,20 @@
     for copy in small:
         copy.start()
 
-    def up_copies(hc):
-        base = 2 * up_units * hc
+    def up_base(step, n):
+        return 2 * feat_units * (hid_chunks * step + n)
+
+    def up_copies(step, n):
+        cut = cut_at(step)
         return [
             pltpu.make_async_copy(
-                src.at[:, :, pl.ds(pl.multiple_of(hc * WIDE, WIDE), WIDE)],
-                ring.at[pl.ds(base + i * up_units, up_units)],
-                ring_sem.at[2 * hc + i],
+                src.at[
+                    pl.ds(cut * feat_units, feat_units),
+                    :,
+                    pl.ds(pl.multiple_of(n * WIDE, WIDE), WIDE),
+                ],
+                ring.at[pl.ds(up_base(step, n) + i * feat_units, feat_units)],
+                ring_sem.at[2 * (hid_chunks * step + n) + i],
             )
             for i, src in enumerate((wg_hbm, wu_hbm))
         ]
@@ -216,17 +226,19 @@
                 pltpu.make_async_copy(
                     wd_hbm.at[:, :, pl.ds(pl.multiple_of(at, half), half)],
                     ring.at[pl.ds(base, down_units), :, pl.ds(side * half, half)],
-                    ring_sem.at[2 * hid_chunks + 2 * k + side],
+                    ring_sem.at[2 * nc * hid_chunks + 2 * k + side],
                 )
             )
         return copies
 
-    def start_up(hc, carry):
-        for copy in up_copies(hc):
-            copy.start()
-        return carry
-
-    lax.fori_loop(0, hid_chunks, start_up, 0)
+    for step in range(nc):
+
+        def start_up(n, carry, step=step):
+            for copy in up_copies(step, n):
+                copy.start()
+            return carry
+
+        lax.fori_loop(0, hid_chunks, start_up, 0)
     ahead = 0
     while ahead < down_chunks and 2 * up_units * hid_chunks + down_units * (ahead + 1) <= SLOTS:
         for copy in down_copies(ahead):
@@ -314,56 +326,64 @@
         along_dev(doff).wait_recv()
         along_cuts(doff, 2).start()
         along_cuts(doff, 1).start()
-        along_cuts(doff - 1, 2).wait_recv()
-        along_cuts(doff - 1, 3).start()
-    along_cuts(nd - 1, 2).wait_recv()
-    along_cuts(nd - 1, 3).start()
-    for doff in range(nd):
-        along_cuts(doff, 1).wait_recv()
-        along_cuts(doff, 3).wait_recv()
-
-    for dd in range(nd):
-        total = jnp.zeros((rows, HD), jnp.float32)
-        for cc in range(nc):
-            xs[dd * rows : (dd + 1) * rows, cc * feat : (cc + 1) * feat] = xrecv[dd, cc, :, :feat]
-            total += xrecv[dd, cc, :, feat:].astype(jnp.float32)
-        square_sum = jnp.sum(total, axis=1, keepdims=True) * (2.0 / HD)
-        scale_v[dd * rows : (dd + 1) * rows, :] = jnp.broadcast_to(
-            lax.rsqrt(square_sum / (nc * feat) + 1e-05), (rows, HD)
-        )
-
-    def up_step(hc, carry):
-        for copy in up_copies(hc):
+
+    def set_scale():
+        for dd in range(nd):
+            total = jnp.zeros((rows, HD), jnp.float32)
+            for cc in range(nc):
+                total += xrecv[dd, cc, :, feat:].astype(jnp.float32)
+            square_sum = jnp.sum(total, axis=1, keepdims=True) * (2.0 / HD)
+            scale_v[dd * rows : (dd + 1) * rows, :] = jnp.broadcast_to(
+                lax.rsqrt(square_sum / (nc * feat) + 1e-05), (rows, HD)
+            )
+
+    def up_step(step, n, carry):
+        for copy in up_copies(step, n):
             copy.wait()
-        base = 2 * up_units * hc
-        scale = scale_v[:, :1]
-        x = xs[...]
+        base = up_base(step, n)
+        columns = pl.ds(pl.multiple_of(n * WIDE, WIDE), WIDE)
+        x = xs[step]
         gate = jnp.dot(
             x,
-            ring[pl.ds(base, up_units)].reshape(up_units * UNIT, WIDE),
+            ring[pl.ds(base, feat_units)].reshape(feat, WIDE),
             preferred_element_type=jnp.float32,
         )
         upper = jnp.dot(
             x,
-            ring[pl.ds(base + up_units, up_units)].reshape(up_units * UNIT, WIDE),
+            ring[pl.ds(base + feat_units, feat_units)].reshape(feat, WIDE),
             preferred_element_type=jnp.float32,
         )
-        gate = gate * scale
-        upper = upper * scale
-        hid[:, pl.ds(pl.multiple_of(hc * WIDE, WIDE), WIDE)] = (
-            gate / (1.0 + jnp.exp(-gate)) * upper
-        ).astype(jnp.bfloat16)
+        if step > 0:
+            gate += gate_v[:, columns]
+            upper += upper_v[:, columns]
+        if step < nc - 1:
+            gate_v[:, columns] = gate
+            upper_v[:, columns] = upper
+        else:
+            scale = scale_v[:, :1]
+            gate = gate * scale
+            upper = upper * scale
+            hid[:, columns] = (gate / (1.0 + jnp.exp(-gate)) * upper).astype(jnp.bfloat16)
         return carry
 
-    done = 0
-    for k in range(ahead, down_chunks):
-        need = -(-(down_slot(k) + down_units) // (2 * up_units))
-        if need > done:
-            lax.fori_loop(done, need, up_step, 0)
-            done = need
-        for copy in down_copies(k):
-            copy.start()
-    lax.fori_loop(done, hid_chunks, up_step, 0)
+    started = ahead
+    for step in range(nc):
+        if step == 1 or step == 3:
+            for doff in range(nd):
+                along_cuts(doff, step).wait_recv()
+        if step == 2:
+            for doff in range(nd):
+                along_cuts(doff, 2).wait_recv()
+                along_cuts(doff, 3).start()
+        if step == nc - 1:
+            set_scale()
+        for dd in range(nd):
+            xs[step, dd * rows : (dd + 1) * rows, :] = xrecv[dd, cut_at(step), :, :feat]
+        lax.fori_loop(0, hid_chunks, functools.partial(up_step, step), 0)
+        while started < down_chunks and down_slot(started) + down_units <= up_base(step + 1, 0):
+            for copy in down_copies(started):
+                copy.start()
+            started += 1
 
     def part_copy(k, side):
         step, sub = down_owner(k, side), k // (nc // 2)
@@ -479,8 +499,10 @@
             pltpu.VMEM((EXPERTS, rows, HD), f32),
             pltpu.VMEM((SLOTS, UNIT, WIDE), bf16),
             pltpu.VMEM((nd, nc, rows, feat + HD), bf16),
-            pltpu.VMEM((total, D), bf16),
+            pltpu.VMEM((nc, total, feat), bf16),
             pltpu.VMEM((total, HD), f32),
+            pltpu.VMEM((total, ff), f32),
+            pltpu.VMEM((total, ff), f32),
             pltpu.VMEM((total, ff), bf16),
             pltpu.VMEM((rows, feat), f32),
             pltpu.VMEM((down_chunks, 2, total, half), bf16),
@@ -488,7 +510,7 @@
             pltpu.VMEM((subs, nd, rows, half), bf16),
             pltpu.VMEM((subs, nd, rows, half), bf16),
             pltpu.SemaphoreType.DMA((8,)),
-            pltpu.SemaphoreType.DMA((2 * hid_chunks + 2 * down_chunks,)),
+            pltpu.SemaphoreType.DMA((2 * nc * hid_chunks + 2 * down_chunks,)),
             pltpu.SemaphoreType.DMA((nd - 1,)),
             pltpu.SemaphoreType.DMA((nd - 1,)),
             pltpu.SemaphoreType.DMA((nc - 1, nd)),

time: 39.5 us -> 39.1 us (0.990)
  Pallas kernels: 37.9 us -> 37.5 us
where the time goes in v3:
time: 39.1 us; the launch traced here: 39 us
  Pallas kernels  37.5 us (96%)
  other arithmetic  1.41 us (4%)
    pallas_call x1, Pallas kernels, shards_fused(): pl.pallas_call(functools.partial(layer_kernel, nd, nc), out_shape=jax.Sha...  37.5 us
    convert_element_type x1, other arithmetic, shards_fused(): return pl.pallas_call(functools.partial(layer_kernel, nd, nc), out_shape=...  1.41 us

profile of v3, /device:TPU:0, one launch (start us, length us, event | category | flops | bytes accessed | tf_op | source)
XLA Modules:
  0.0 39.0 jit_solution(10598209709024203865)
XLA Ops:
  0.0 37.5 %shard_map.109 = f32[16,768]{1,0:T(8,128)} custom-call(bf16[16,768]{1,0:T(8,128)(2,1)} %res_hbm.1, bf16[16,768]{1,0:T(8,128)(2,1)} %q_hbm.1, bf16[16,32,128]{2,1,0:T(8,128)(2,1)} %k_hbm.1, bf16[16,32,128]{2,1,0:T(8,128)(2,1)} %v_hbm.1, s32[16]{0:T(128)} %len_hbm.1, f32[768]{0:T(1024)} %gain_hbm.1, s32[2,16]{1,0:T(2,128)} %bitcast.8, f32[2,16]{1,0:T(2,128)} %bitcast.9, ...), custom_call_target="tpu_custom_call" | custom-call | flops 4831838208 | bytes 75497472 | tf_op jit(solution)/shard_map/pallas_call | solution.py:485
  37.5 1.4 %convert_element_type.3 = bf16[16,768]{1,0:T(8,128)(2,1)} convert(f32[16,768]{1,0:T(8,128)} %shard_map.109) | non-fusion elementwise | flops 12288 | bytes 73728 | tf_op jit(solution)/shard_map/convert_element_type | solution.py:541

commit v4 on v3

--- a/solution.py
+++ b/solution.py
@@ -130,6 +130,7 @@
     cutrecv,
     summed,
     back,
+    last_back,
     small_sem,
     ring_sem,
     dev_send,
@@ -138,6 +139,8 @@
     cut_recv,
     part_send,
     part_recv,
+    last_send,
+    last_recv,
     sum_send,
     sum_recv,
 ):
@@ -165,12 +168,16 @@
     def on_dev(doff):
         return {"dev": lax.rem(d + doff, nd), "cuts": c}
 
+    def on_mate(doff):
+        return {"dev": lax.rem(d + doff, nd), "cuts": mate}
+
     def on_cut(step):
         return {"dev": d, "cuts": cut_at(step)}
 
     barrier = pltpu.get_barrier_semaphore()
     for doff in range(1, nd):
         pl.semaphore_signal(barrier, inc=1, device_id=on_dev(doff), device_id_type=MESH)
+        pl.semaphore_signal(barrier, inc=1, device_id=on_mate(doff), device_id_type=MESH)
     for step in range(1, nc):
         pl.semaphore_signal(barrier, inc=1, device_id=on_cut(step), device_id_type=MESH)
 
@@ -215,13 +222,13 @@
         return unit % SLOTS
 
     def down_owner(k, side):
-        return nc - 2 - 2 * (k % (nc // 2)) + side
+        return nc - 2 - 2 * (k // subs) + side
 
     def down_copies(k):
         base = down_slot(k)
         copies = []
         for side in range(2):
-            at = cut_at(down_owner(k, side)) * feat + (k // (nc // 2)) * half
+            at = cut_at(down_owner(k, side)) * feat + (k % subs) * half
             copies.append(
                 pltpu.make_async_copy(
                     wd_hbm.at[:, :, pl.ds(pl.multiple_of(at, half), half)],
@@ -288,7 +295,7 @@
     xrecv[d, c, :, pl.ds(0, feat)] = (mixed * gain_v[...].reshape(1, feat)).astype(jnp.bfloat16)
     xrecv[d, c, :, pl.ds(feat, HD)] = parts.astype(jnp.bfloat16)
 
-    pl.semaphore_wait(barrier, nd + nc - 2)
+    pl.semaphore_wait(barrier, 2 * (nd - 1) + nc - 1)
 
     def along_dev(doff):
         return pltpu.make_async_remote_copy(
@@ -386,7 +393,7 @@
             started += 1
 
     def part_copy(k, side):
-        step, sub = down_owner(k, side), k // (nc // 2)
+        step, sub = down_owner(k, side), k % subs
         return pltpu.make_async_remote_copy(
             src_ref=outbuf.at[k, side],
             dst_ref=cutrecv.at[sub, step - 1],
@@ -406,13 +413,29 @@
             device_id_type=MESH,
         )
 
+    def last_copy(doff):
+        return pltpu.make_async_remote_copy(
+            src_ref=outbuf.at[
+                down_chunks - 1, 1, pl.ds(pl.multiple_of(lax.rem(d + doff, nd) * rows, rows), rows)
+            ],
+            dst_ref=last_back.at[d],
+            send_sem=last_send.at[doff],
+            recv_sem=last_recv.at[doff],
+            device_id=on_mate(doff),
+            device_id_type=MESH,
+        )
+
     def far_parts(k):
-        return [side for side in range(2) if down_owner(k, side) != 0]
+        return [
+            side
+            for side in range(2)
+            if down_owner(k, side) != 0 and (k, side) != (down_chunks - 1, 1)
+        ]
 
     def add_parts(sub):
-        last = sub * (nc // 2) + nc // 2 - 1
+        last = (nc // 2 - 1) * subs + sub
         total = outbuf[last, 0].astype(jnp.float32)
-        for k in range(last + 1 - nc // 2, last + 1):
+        for k in range(sub, down_chunks, subs):
             for side in far_parts(k):
                 part_copy(k, side).wait_recv()
                 total += cutrecv[sub, down_owner(k, side) - 1].astype(jnp.float32)
@@ -433,16 +456,26 @@
             outbuf[k, side] = acc[:, side * half : (side + 1) * half]
         for side in far_parts(k):
             part_copy(k, side).start()
-        if k >= nc // 2 and k % (nc // 2) == 0:
-            add_parts(k // (nc // 2) - 1)
-    add_parts(subs - 1)
+        if k == down_chunks - 1:
+            for doff in range(1, nd):
+                last_copy(doff).start()
+            last_copy(0).start()
+            add_parts(subs - 1)
+        if k > (nc // 2 - 1) * subs:
+            add_parts(k - (nc // 2 - 1) * subs - 1)
 
     for sub in range(subs):
         total = mixed_v[:, sub * half : (sub + 1) * half]
         for doff in range(1, nd):
             sum_copy(sub, doff).wait_recv()
+        if sub == subs - 1:
+            for doff in range(nd):
+                last_copy(doff).wait_recv()
         for dd in range(nd):
-            total += chosen_v[dd, :, :1] * back[sub, dd].astype(jnp.float32)
+            part = back[sub, dd].astype(jnp.float32)
+            if sub == subs - 1:
+                part += last_back[dd].astype(jnp.float32)
+            total += chosen_v[dd, :, :1] * part
         out_ref[:, sub * half : (sub + 1) * half] = total
 
     for doff in range(1, nd):
@@ -453,6 +486,8 @@
     for k in range(down_chunks):
         for side in far_parts(k):
             part_copy(k, side).wait_send()
+    for doff in range(nd):
+        last_copy(doff).wait_send()
     for sub in range(subs):
         for doff in range(1, nd):
             sum_copy(sub, doff).wait_send()
@@ -509,6 +544,7 @@
             pltpu.VMEM((subs, nc - 1, total, half), bf16),
             pltpu.VMEM((subs, nd, rows, half), bf16),
             pltpu.VMEM((subs, nd, rows, half), bf16),
+            pltpu.VMEM((nd, rows, half), bf16),
             pltpu.SemaphoreType.DMA((8,)),
             pltpu.SemaphoreType.DMA((2 * nc * hid_chunks + 2 * down_chunks,)),
             pltpu.SemaphoreType.DMA((nd - 1,)),
@@ -517,6 +553,8 @@
             pltpu.SemaphoreType.DMA((nc - 1, nd)),
             pltpu.SemaphoreType.DMA((subs, nc - 1)),
             pltpu.SemaphoreType.DMA((subs, nc - 1)),
+            pltpu.SemaphoreType.DMA((nd,)),
+            pltpu.SemaphoreType.DMA((nd,)),
             pltpu.SemaphoreType.DMA((subs, nd - 1)),
             pltpu.SemaphoreType.DMA((subs, nd - 1)),
         ],

time: 39.1 us -> 37 us (0.946)
  Pallas kernels: 37.5 us -> 35.4 us
    pallas_call x1, Pallas kernels: 37.5 us -> 35.4 us  [shards_fused(): pl.pallas_call(functools.partial(layer_kernel, nd, nc), out_shape=jax.Sha...]
where the time goes in v4:
time: 37 us; the launch traced here: 36.8 us
  Pallas kernels  35.4 us (96%)
  other arithmetic  1.41 us (4%)
    pallas_call x1, Pallas kernels, shards_fused(): pl.pallas_call(functools.partial(layer_kernel, nd, nc), out_shape=jax.Sha...  35.4 us
    convert_element_type x1, other arithmetic, shards_fused(): return pl.pallas_call(functools.partial(layer_kernel, nd, nc), out_shape=...  1.41 us

profile of v4, /device:TPU:0, one launch (start us, length us, event | category | flops | bytes accessed | tf_op | source)
XLA Modules:
  0.0 36.8 jit_solution(14598803741041490984)
XLA Ops:
  0.0 35.4 %shard_map.109 = f32[16,768]{1,0:T(8,128)} custom-call(bf16[16,768]{1,0:T(8,128)(2,1)} %res_hbm.1, bf16[16,768]{1,0:T(8,128)(2,1)} %q_hbm.1, bf16[16,32,128]{2,1,0:T(8,128)(2,1)} %k_hbm.1, bf16[16,32,128]{2,1,0:T(8,128)(2,1)} %v_hbm.1, s32[16]{0:T(128)} %len_hbm.1, f32[768]{0:T(1024)} %gain_hbm.1, s32[2,16]{1,0:T(2,128)} %bitcast.8, f32[2,16]{1,0:T(2,128)} %bitcast.9, ...), custom_call_target="tpu_custom_call" | custom-call | flops 4831838208 | bytes 75497472 | tf_op jit(solution)/shard_map/pallas_call | solution.py:520
  35.4 1.4 %convert_element_type.3 = bf16[16,768]{1,0:T(8,128)(2,1)} convert(f32[16,768]{1,0:T(8,128)} %shard_map.109) | non-fusion elementwise | flops 12288 | bytes 73728 | tf_op jit(solution)/shard_map/convert_element_type | solution.py:579
